TPU v7x, 128 devices: a whole 4x4x4 slice. The times are simulated.
128 devices in a mesh: wall: 4 (over y), span: 32 (over x, z, core).
Axes of the slice: x: 4, y: 4, z: 4, core: 2. Of those that a mesh axis runs over, the one named last changes fastest.
Arguments:
- jac_lower: bfloat16 [8, 112, 112, 4096], P('wall', None, None, 'span')
- jac_inv_diag: bfloat16 [8, 112, 112, 4096], P('wall', None, None, 'span')
- jac_upper: bfloat16 [8, 112, 112, 4096], P('wall', None, None, 'span')
- residual: float32 [8, 112, 4096], P('wall', None, 'span'), may hold values from -6 to 6
- prev_update: float32 [8, 112, 4096], P('wall', None, 'span'), may hold values from -6 to 6
- send_lines: int32 [32, 32, 64], P('span'), may hold values from 0 to 127
- send_count: int32 [32, 32], P('span'), may hold values from 1 to 64, as said below
- recv_lines: int32 [32, 32, 64], P('span'), may hold values from 0 to 127
- active_lines: int32 [32], P('span'), may hold values from 64 to 128, as said below
Outputs:
- line_update: float32 [8, 112, 4096], P('wall', None, 'span')
Inputs may be any that keep to these rules, and one draw needn't show every extreme that they name: `send_count`: every sender fills all 64 slots towards at least one receiver, and one receiver gets full slots from every sender. `active_lines`: at least one device has all 128 lines live.
All inputs are finite; a program needn't handle non-finite values.
Results may differ from a plain program's by a relative error of at most 0.0003.
Values sent between devices are 32-bit elements; how exact they have to be, the bound alone decides.
A program may use at most 256 MiB of HBM per device.

v0:
```python
import jax
import jax.numpy as jnp
from jax import lax
from jax.sharding import PartitionSpec as P


def from_behind(value, axis, steps):
    count = lax.axis_size(axis)
    first, last = (max(0, -steps), min(count, count - steps))
    return lax.ppermute(value, axis, [(source, source + steps) for source in range(first, last)])


def matvec(block, vec):
    return jnp.einsum("abl,bl->al", block.astype(jnp.float32), vec, precision=lax.Precision.HIGHEST)


def lower_sweep(jac_lower, rhs, start_vec):

    def lower_step(carry, inputs):
        block, right = inputs
        value = right - matvec(block, carry)
        return (value, value)

    return lax.scan(lower_step, start_vec, (jac_lower, rhs))


def upper_sweep(jac_inv_diag, jac_upper, values, start_vec):

    def upper_step(carry, inputs):
        inverse, block, right = inputs
        value = matvec(inverse, right - matvec(block, carry))
        return (value, value)

    return lax.scan(upper_step, start_vec, (jac_inv_diag, jac_upper, values), reverse=True)


def local(
    jac_lower,
    jac_inv_diag,
    jac_upper,
    residual,
    prev_update,
    send_lines,
    send_count,
    recv_lines,
    active_lines,
):
    cells, width, _, lanes = jac_lower.shape
    spans = lax.axis_size("span")
    slot_count = send_lines.shape[2]
    lane_ids = jnp.arange(lanes, dtype=jnp.int32)
    slot_ids = jnp.arange(slot_count, dtype=jnp.int32)
    tiles = prev_update.reshape(cells * width, lanes)
    keep = (slot_ids[None, :] < send_count[0][:, None]) & (send_lines[0] < active_lines[0])
    picks = (lane_ids[:, None] == send_lines[0].reshape(-1)[None, :]) & keep.reshape(-1)[None, :]
    outgoing = jnp.dot(tiles, picks.astype(jnp.float32), precision=lax.Precision.HIGHEST)
    outgoing = outgoing.reshape(cells * width, spans, slot_count)
    incoming = lax.all_to_all(outgoing, "span", split_axis=1, concat_axis=1, tiled=True)
    landing = (recv_lines[0].reshape(-1)[:, None] == lane_ids[None, :]).astype(jnp.float32)
    coupling = jnp.dot(
        incoming.reshape(cells * width, spans * slot_count),
        landing,
        precision=lax.Precision.HIGHEST,
    )
    live = (lane_ids < active_lines[0]).astype(jnp.float32)
    rhs = (residual - coupling.reshape(cells, width, lanes)) * live[None, None, :]
    zero_vec = jnp.zeros((width, lanes), jnp.float32)
    entering = zero_vec
    for turn in range(lax.axis_size("wall") - 1):
        last, values = lower_sweep(jac_lower, rhs, entering)
        entering = from_behind(last, "wall", 1)
    last, values = lower_sweep(jac_lower, rhs, entering)
    leaving = zero_vec
    for turn in range(lax.axis_size("wall") - 1):
        first, result = upper_sweep(jac_inv_diag, jac_upper, values, leaving)
        leaving = from_behind(first, "wall", -1)
    first, result = upper_sweep(jac_inv_diag, jac_upper, values, leaving)
    return result


def solution(mesh):
    return jax.shard_map(
        local,
        mesh=mesh,
        in_specs=(
            P("wall", None, None, "span"),
            P("wall", None, None, "span"),
            P("wall", None, None, "span"),
            P("wall", None, "span"),
            P("wall", None, "span"),
            P("span", None, None),
            P("span", None),
            P("span", None, None),
            P("span"),
        ),
        out_specs=P("wall", None, "span"),
        check_vma=False,
    )
```

profile of v0, /device:TPU:16, one launch (start us, length us, event | category | flops | bytes accessed | tf_op | source)
XLA Modules:
  0.0 157.9 jit_solution(12267908807093458648)
XLA Ops:
  5.1 8.3 %all-to-all-start = ((f32[224,32,64]{0,2,1:T(8,128)}), f32[224,32,64]{0,2,1:T(8,128)}, u32[]{:S(2)}, u32[]{:S(2)}) async-start(f32[224,32,64]{0,2,1:T(8,128)} %bitcast.70), calls=%async_computation | async-start | bytes 4194304 | tf_op jit(solution)/shard_map/all_to_all | solution.py:58
  13.4 28.8 %all-to-all-done = f32[224,32,64]{0,2,1:T(8,128)} async-done(((f32[224,32,64]{0,2,1:T(8,128)}), f32[224,32,64]{0,2,1:T(8,128)}, u32[]{:S(2)}, u32[]{:S(2)}) %all-to-all-start) | async-done | bytes 1835040 | tf_op jit(solution)/shard_map/all_to_all | solution.py:58
  42.3 2.6 %dot_general.72 = f32[2,112,2048]{1,0,2:T(2,128)S(1)} reshape(f32[224,32,64]{0,2,1:T(8,128)} %all-to-all-done) | data formatting | bytes 3670016 | tf_op jit(solution)/shard_map/dot_general | solution.py:60
  44.9 2.1 %fusion.9 = f32[2,112,128]{2,1,0:T(8,128)S(1)} fusion(f32[2,112,128]{2,1,0:T(8,128)S(1)} %copy-done.2, f32[2,112,2048]{1,0,2:T(2,128)S(1)} %dot_general.72, s32[2048]{0:T(1024)S(1)} %eq.34, f32[128]{0:T(128)S(1)} %compare_convert_fusion), kind=kOutput, calls=%fused_computation.31 | convolution fusion | flops 704962560 | bytes 2073088 | tf_op jit(solution)/shard_map/dot_general | solution.py:60
  47.0 6.1 %while.108 = (s32[]{:T(128)}, f32[112,128]{1,0:T(8,128)S(1)}, f32[2,112,128]{2,1,0:T(8,128)S(1)}, bf16[2,112,112,128]{3,2,1,0:T(8,128)(2,1)}, s32[]{:T(128)}, /*index=5*/s32[]{:T(128)}) while((s32[]{:T(128)}, f32[112,128]{1,0:T(8,128)S(1)}, f32[2,112,128]{2,1,0:T(8,128)S(1)}, bf16[2,112,112,128]{3,2,1,0:T(8,128)(2,1)}, s32[]{:T(128)}, ...), condition=%wide.region_1.2_spmd.clone, body=%wide.region_0.1_spmd.clone.sunk | while | flops 4831235 | bytes 3612759 | solution.py:24
  47.0 3.0 %multiply_reduce_fusion.35 = f32[128,112]{0,1:T(8,128)S(1)} fusion(f32[128,112]{0,1:T(8,128)S(1)} %select_bitcast_fusion.2, bf16[2,112,112,128]{3,2,1,0:T(8,128)(2,1)} %get-tuple-element.885, s32[]{:T(128)} %get-tuple-element.876), kind=kLoop, calls=%fused_computation.24.clone.1 | loop fusion | flops 4802560 | bytes 3325956 | tf_op jit(solution)/shard_map/while/body/eval_jaxpr/abl,bl->al/dot_general | solution.py:14
  50.1 3.0 %multiply_reduce_fusion.35 = f32[128,112]{0,1:T(8,128)S(1)} fusion(f32[128,112]{0,1:T(8,128)S(1)} %select_bitcast_fusion.2, bf16[2,112,112,128]{3,2,1,0:T(8,128)(2,1)} %get-tuple-element.885, s32[]{:T(128)} %get-tuple-element.876), kind=kLoop, calls=%fused_computation.24.clone.1 | loop fusion | flops 4802560 | bytes 3325956 | tf_op jit(solution)/shard_map/while/body/eval_jaxpr/abl,bl->al/dot_general | solution.py:14
  53.1 3.2 %collective-permute-start = (f32[112,128]{1,0:T(8,128)S(1)}, f32[112,128]{1,0:T(8,128)S(1)}, u32[]{:S(2)}, u32[]{:S(2)}) collective-permute-start(f32[112,128]{1,0:T(8,128)S(1)} %get-tuple-element.529), channel_id=1, source_target_pairs={{0,32},{32,64},{64,96},{1,33},{33,65},{65,97},{2,34},{34,66},{66,9... | collective-permute-start | bytes 172040 | tf_op jit(solution)/shard_map/ppermute | solution.py:10
  56.3 2.9 %collective-permute-done = f32[112,128]{1,0:T(8,128)S(1)} collective-permute-done((f32[112,128]{1,0:T(8,128)S(1)}, f32[112,128]{1,0:T(8,128)S(1)}, u32[]{:S(2)}, u32[]{:S(2)}) %collective-permute-start) | collective-permute-done | bytes 57376 | tf_op jit(solution)/shard_map/ppermute | solution.py:10
  59.2 6.0 %while.101 = (s32[]{:T(128)}, f32[112,128]{1,0:T(8,128)S(1)}, f32[2,112,128]{2,1,0:T(8,128)S(1)}, bf16[2,112,112,128]{3,2,1,0:T(8,128)(2,1)}, s32[]{:T(128)}) while((s32[]{:T(128)}, f32[112,128]{1,0:T(8,128)S(1)}, f32[2,112,128]{2,1,0:T(8,128)S(1)}, bf16[2,112,112,128]{3,2,1,0:T(8,128)(2,1)}, s32[]{:T(128)}) %tuple.213), condition=%wide.region_3.4_spmd, body=%wide.region_2.3_spmd.sunk | while | flops 4816898 | bytes 3498053 | solution.py:24
  59.2 3.0 %multiply_reduce_fusion.24 = f32[128,112]{0,1:T(8,128)S(1)} fusion(f32[128,112]{0,1:T(8,128)S(1)} %bitcast.228, bf16[2,112,112,128]{3,2,1,0:T(8,128)(2,1)} %get-tuple-element.901, s32[]{:T(128)} %get-tuple-element.893), kind=kLoop, calls=%fused_computation.clone.1 | loop fusion | flops 4802560 | bytes 3325956 | tf_op jit(solution)/shard_map/while/body/eval_jaxpr/abl,bl->al/dot_general | solution.py:14
  62.2 3.0 %multiply_reduce_fusion.24 = f32[128,112]{0,1:T(8,128)S(1)} fusion(f32[128,112]{0,1:T(8,128)S(1)} %bitcast.228, bf16[2,112,112,128]{3,2,1,0:T(8,128)(2,1)} %get-tuple-element.901, s32[]{:T(128)} %get-tuple-element.893), kind=kLoop, calls=%fused_computation.clone.1 | loop fusion | flops 4802560 | bytes 3325956 | tf_op jit(solution)/shard_map/while/body/eval_jaxpr/abl,bl->al/dot_general | solution.py:14
  65.2 3.2 %collective-permute-start.1 = (f32[112,128]{1,0:T(8,128)S(1)}, f32[112,128]{1,0:T(8,128)S(1)}, u32[]{:S(2)}, u32[]{:S(2)}) collective-permute-start(f32[112,128]{1,0:T(8,128)S(1)} %get-tuple-element.530), channel_id=1, source_target_pairs={{0,32},{32,64},{64,96},{1,33},{33,65},{65,97},{2,34},{34,66},{66,9... | collective-permute-start | bytes 172040 | tf_op jit(solution)/shard_map/ppermute | solution.py:10
  68.4 2.9 %collective-permute-done.1 = f32[112,128]{1,0:T(8,128)S(1)} collective-permute-done((f32[112,128]{1,0:T(8,128)S(1)}, f32[112,128]{1,0:T(8,128)S(1)}, u32[]{:S(2)}, u32[]{:S(2)}) %collective-permute-start.1) | collective-permute-done | bytes 57376 | tf_op jit(solution)/shard_map/ppermute | solution.py:10
  71.3 6.0 %while.102 = (s32[]{:T(128)}, f32[112,128]{1,0:T(8,128)S(1)}, f32[2,112,128]{2,1,0:T(8,128)S(1)}, bf16[2,112,112,128]{3,2,1,0:T(8,128)(2,1)}, s32[]{:T(128)}) while((s32[]{:T(128)}, f32[112,128]{1,0:T(8,128)S(1)}, f32[2,112,128]{2,1,0:T(8,128)S(1)}, bf16[2,112,112,128]{3,2,1,0:T(8,128)(2,1)}, s32[]{:T(128)}) %tuple.214), condition=%wide.region_5.6_spmd, body=%wide.region_4.5_spmd.sunk | while | flops 4816898 | bytes 3498053 | solution.py:24
  71.3 3.0 %multiply_reduce_fusion.25 = f32[128,112]{0,1:T(8,128)S(1)} fusion(f32[128,112]{0,1:T(8,128)S(1)} %bitcast.229, bf16[2,112,112,128]{3,2,1,0:T(8,128)(2,1)} %get-tuple-element.916, s32[]{:T(128)} %get-tuple-element.908), kind=kLoop, calls=%fused_computation.2.clone.1 | loop fusion | flops 4802560 | bytes 3325956 | tf_op jit(solution)/shard_map/while/body/eval_jaxpr/abl,bl->al/dot_general | solution.py:14
  74.3 3.0 %multiply_reduce_fusion.25 = f32[128,112]{0,1:T(8,128)S(1)} fusion(f32[128,112]{0,1:T(8,128)S(1)} %bitcast.229, bf16[2,112,112,128]{3,2,1,0:T(8,128)(2,1)} %get-tuple-element.916, s32[]{:T(128)} %get-tuple-element.908), kind=kLoop, calls=%fused_computation.2.clone.1 | loop fusion | flops 4802560 | bytes 3325956 | tf_op jit(solution)/shard_map/while/body/eval_jaxpr/abl,bl->al/dot_general | solution.py:14
  77.3 3.2 %collective-permute-start.2 = (f32[112,128]{1,0:T(8,128)S(1)}, f32[112,128]{1,0:T(8,128)S(1)}, u32[]{:S(2)}, u32[]{:S(2)}) collective-permute-start(f32[112,128]{1,0:T(8,128)S(1)} %get-tuple-element.531), channel_id=1, source_target_pairs={{0,32},{32,64},{64,96},{1,33},{33,65},{65,97},{2,34},{34,66},{66,9... | collective-permute-start | bytes 172040 | tf_op jit(solution)/shard_map/ppermute | solution.py:10
  80.5 2.9 %collective-permute-done.2 = f32[112,128]{1,0:T(8,128)S(1)} collective-permute-done((f32[112,128]{1,0:T(8,128)S(1)}, f32[112,128]{1,0:T(8,128)S(1)}, u32[]{:S(2)}, u32[]{:S(2)}) %collective-permute-start.2) | collective-permute-done | bytes 57376 | tf_op jit(solution)/shard_map/ppermute | solution.py:10
  83.4 6.1 %while.103 = (s32[]{:T(128)}, f32[112,128]{1,0:T(8,128)S(1)}, f32[2,112,128]{2,1,0:T(8,128)S(1)}, f32[2,112,128]{2,1,0:T(8,128)S(1)}, bf16[2,112,112,128]{3,2,1,0:T(8,128)(2,1)}, /*index=5*/s32[]{:T(128)}) while((s32[]{:T(128)}, f32[112,128]{1,0:T(8,128)S(1)}, f32[2,112,128]{2,1,0:T(8,128)S(1)}, f32[2,112,128]{2,1,0:T(8,128)S(1)}, ...), condition=%wide.region_7.8_spmd, body=%wide.region_6.7_spmd.sunk | while | flops 4816898 | bytes 3555405 | solution.py:24
  83.4 3.0 %multiply_reduce_fusion.26 = f32[128,112]{0,1:T(8,128)S(1)} fusion(f32[128,112]{0,1:T(8,128)S(1)} %bitcast.227, bf16[2,112,112,128]{3,2,1,0:T(8,128)(2,1)} %get-tuple-element.934, s32[]{:T(128)} %get-tuple-element.924), kind=kLoop, calls=%fused_computation.4.clone.1 | loop fusion | flops 4802560 | bytes 3325956 | tf_op jit(solution)/shard_map/while/body/eval_jaxpr/abl,bl->al/dot_general | solution.py:14
  86.5 3.0 %multiply_reduce_fusion.26 = f32[128,112]{0,1:T(8,128)S(1)} fusion(f32[128,112]{0,1:T(8,128)S(1)} %bitcast.227, bf16[2,112,112,128]{3,2,1,0:T(8,128)(2,1)} %get-tuple-element.934, s32[]{:T(128)} %get-tuple-element.924), kind=kLoop, calls=%fused_computation.4.clone.1 | loop fusion | flops 4802560 | bytes 3325956 | tf_op jit(solution)/shard_map/while/body/eval_jaxpr/abl,bl->al/dot_general | solution.py:14
  89.5 12.4 %while.104 = (s32[]{:T(128)}, f32[112,128]{0,1:T(8,128)S(1)}, f32[2,112,128]{2,1,0:T(8,128)S(1)}, bf16[2,112,112,128]{3,2,1,0:T(8,128)(2,1)}, bf16[2,112,112,128]{3,2,1,0:T(8,128)(2,1)}, /*index=5*/s32[]{:T(128)}) while((s32[]{:T(128)}, f32[112,128]{0,1:T(8,128)S(1)}, f32[2,112,128]{2,1,0:T(8,128)S(1)}, bf16[2,112,112,128]{3,2,1,0:T(8,128)(2,1)}, ...), condition=%wide.region_9.10_spmd, body=%wide.region_8.9_spmd.sunk | while | flops 9619459 | bytes 7053405 | solution.py:34
  89.6 3.0 %multiply_reduce_fusion.27 = f32[128,112]{0,1:T(8,128)S(1)} fusion(f32[128,112]{0,1:T(8,128)S(1)} %copy.119, bf16[2,112,112,128]{3,2,1,0:T(8,128)(2,1)} %get-tuple-element.951, s32[]{:T(128)S(6)} %sub.115), kind=kLoop, calls=%fused_computation.8.clone.1 | loop fusion | flops 4802560 | bytes 3325956 | tf_op jit(solution)/shard_map/while/body/eval_jaxpr/abl,bl->al/dot_general | solution.py:14
  92.6 3.0 %multiply_reduce_fusion.28 = f32[128,112]{0,1:T(8,128)S(1)} fusion(f32[128,112]{0,1:T(8,128)S(1)} %fusion.24, bf16[2,112,112,128]{3,2,1,0:T(8,128)(2,1)} %get-tuple-element.952, s32[]{:T(128)S(6)} %sub.115), kind=kLoop, calls=%fused_computation.7.clone.1 | loop fusion | flops 4802560 | bytes 3325956 | tf_op jit(solution)/shard_map/while
  95.8 3.0 %multiply_reduce_fusion.27 = f32[128,112]{0,1:T(8,128)S(1)} fusion(f32[128,112]{0,1:T(8,128)S(1)} %copy.119, bf16[2,112,112,128]{3,2,1,0:T(8,128)(2,1)} %get-tuple-element.951, s32[]{:T(128)S(6)} %sub.115), kind=kLoop, calls=%fused_computation.8.clone.1 | loop fusion | flops 4802560 | bytes 3325956 | tf_op jit(solution)/shard_map/while/body/eval_jaxpr/abl,bl->al/dot_general | solution.py:14
  98.8 3.0 %multiply_reduce_fusion.28 = f32[128,112]{0,1:T(8,128)S(1)} fusion(f32[128,112]{0,1:T(8,128)S(1)} %fusion.24, bf16[2,112,112,128]{3,2,1,0:T(8,128)(2,1)} %get-tuple-element.952, s32[]{:T(128)S(6)} %sub.115), kind=kLoop, calls=%fused_computation.7.clone.1 | loop fusion | flops 4802560 | bytes 3325956 | tf_op jit(solution)/shard_map/while
  101.9 2.5 %collective-permute-start.3 = (f32[112,128]{0,1:T(8,128)S(1)}, f32[112,128]{0,1:T(8,128)S(1)}, u32[]{:S(2)}, u32[]{:S(2)}) collective-permute-start(f32[112,128]{0,1:T(8,128)S(1)} %get-tuple-element.533), channel_id=1, source_target_pairs={{32,0},{64,32},{96,64},{33,1},{65,33},{97,65},{34,2},{66,34},{98,6... | collective-permute-start | bytes 172040 | tf_op jit(solution)/shard_map/ppermute | solution.py:10
  104.5 3.6 %collective-permute-done.3 = f32[112,128]{0,1:T(8,128)S(1)} collective-permute-done((f32[112,128]{0,1:T(8,128)S(1)}, f32[112,128]{0,1:T(8,128)S(1)}, u32[]{:S(2)}, u32[]{:S(2)}) %collective-permute-start.3) | collective-permute-done | bytes 57376 | tf_op jit(solution)/shard_map/ppermute | solution.py:10
  108.1 12.4 %while.105 = (s32[]{:T(128)}, f32[112,128]{0,1:T(8,128)S(1)}, f32[2,112,128]{2,1,0:T(8,128)S(1)}, bf16[2,112,112,128]{3,2,1,0:T(8,128)(2,1)}, bf16[2,112,112,128]{3,2,1,0:T(8,128)(2,1)}, /*index=5*/s32[]{:T(128)}) while((s32[]{:T(128)}, f32[112,128]{0,1:T(8,128)S(1)}, f32[2,112,128]{2,1,0:T(8,128)S(1)}, ...), condition=%wide.region_11.12_spmd, body=%wide.region_10.11_spmd.sunk | while | flops 9619459 | bytes 7053405 | solution.py:34
  108.2 3.0 %multiply_reduce_fusion.29 = f32[128,112]{0,1:T(8,128)S(1)} fusion(f32[128,112]{0,1:T(8,128)S(1)} %copy.121, bf16[2,112,112,128]{3,2,1,0:T(8,128)(2,1)} %get-tuple-element.969, s32[]{:T(128)S(6)} %sub.117), kind=kLoop, calls=%fused_computation.12.clone.1 | loop fusion | flops 4802560 | bytes 3325956 | tf_op jit(solution)/shard_map/while/body/eval_jaxpr/abl,bl->al/dot_general | solution.py:14
  111.2 3.0 %multiply_reduce_fusion.30 = f32[128,112]{0,1:T(8,128)S(1)} fusion(f32[128,112]{0,1:T(8,128)S(1)} %fusion.25, bf16[2,112,112,128]{3,2,1,0:T(8,128)(2,1)} %get-tuple-element.970, s32[]{:T(128)S(6)} %sub.117), kind=kLoop, calls=%fused_computation.11.clone.1 | loop fusion | flops 4802560 | bytes 3325956 | tf_op jit(solution)/shard_map/while
  114.4 3.0 %multiply_reduce_fusion.29 = f32[128,112]{0,1:T(8,128)S(1)} fusion(f32[128,112]{0,1:T(8,128)S(1)} %copy.121, bf16[2,112,112,128]{3,2,1,0:T(8,128)(2,1)} %get-tuple-element.969, s32[]{:T(128)S(6)} %sub.117), kind=kLoop, calls=%fused_computation.12.clone.1 | loop fusion | flops 4802560 | bytes 3325956 | tf_op jit(solution)/shard_map/while/body/eval_jaxpr/abl,bl->al/dot_general | solution.py:14
  117.4 3.0 %multiply_reduce_fusion.30 = f32[128,112]{0,1:T(8,128)S(1)} fusion(f32[128,112]{0,1:T(8,128)S(1)} %fusion.25, bf16[2,112,112,128]{3,2,1,0:T(8,128)(2,1)} %get-tuple-element.970, s32[]{:T(128)S(6)} %sub.117), kind=kLoop, calls=%fused_computation.11.clone.1 | loop fusion | flops 4802560 | bytes 3325956 | tf_op jit(solution)/shard_map/while
  120.5 2.4 %collective-permute-start.4 = (f32[112,128]{0,1:T(8,128)S(1)}, f32[112,128]{0,1:T(8,128)S(1)}, u32[]{:S(2)}, u32[]{:S(2)}) collective-permute-start(f32[112,128]{0,1:T(8,128)S(1)} %get-tuple-element.534), channel_id=1, source_target_pairs={{32,0},{64,32},{96,64},{33,1},{65,33},{97,65},{34,2},{66,34},{98,6... | collective-permute-start | bytes 172040 | tf_op jit(solution)/shard_map/ppermute | solution.py:10
  122.8 3.8 %collective-permute-done.4 = f32[112,128]{0,1:T(8,128)S(1)} collective-permute-done((f32[112,128]{0,1:T(8,128)S(1)}, f32[112,128]{0,1:T(8,128)S(1)}, u32[]{:S(2)}, u32[]{:S(2)}) %collective-permute-start.4) | collective-permute-done | bytes 57376 | tf_op jit(solution)/shard_map/ppermute | solution.py:10
  126.6 12.4 %while.106 = (s32[]{:T(128)}, f32[112,128]{0,1:T(8,128)S(1)}, f32[2,112,128]{2,1,0:T(8,128)S(1)}, bf16[2,112,112,128]{3,2,1,0:T(8,128)(2,1)}, bf16[2,112,112,128]{3,2,1,0:T(8,128)(2,1)}, /*index=5*/s32[]{:T(128)}) while((s32[]{:T(128)}, f32[112,128]{0,1:T(8,128)S(1)}, f32[2,112,128]{2,1,0:T(8,128)S(1)}, ...), condition=%wide.region_13.14_spmd, body=%wide.region_12.13_spmd.sunk | while | flops 9619459 | bytes 7053405 | solution.py:34
  126.7 3.0 %multiply_reduce_fusion.31 = f32[128,112]{0,1:T(8,128)S(1)} fusion(f32[128,112]{0,1:T(8,128)S(1)} %copy.123, bf16[2,112,112,128]{3,2,1,0:T(8,128)(2,1)} %get-tuple-element.987, s32[]{:T(128)S(6)} %sub.119), kind=kLoop, calls=%fused_computation.16.clone.1 | loop fusion | flops 4802560 | bytes 3325956 | tf_op jit(solution)/shard_map/while/body/eval_jaxpr/abl,bl->al/dot_general | solution.py:14
  129.7 3.0 %multiply_reduce_fusion.32 = f32[128,112]{0,1:T(8,128)S(1)} fusion(f32[128,112]{0,1:T(8,128)S(1)} %fusion.26, bf16[2,112,112,128]{3,2,1,0:T(8,128)(2,1)} %get-tuple-element.988, s32[]{:T(128)S(6)} %sub.119), kind=kLoop, calls=%fused_computation.15.clone.1 | loop fusion | flops 4802560 | bytes 3325956 | tf_op jit(solution)/shard_map/while
  132.9 3.0 %multiply_reduce_fusion.31 = f32[128,112]{0,1:T(8,128)S(1)} fusion(f32[128,112]{0,1:T(8,128)S(1)} %copy.123, bf16[2,112,112,128]{3,2,1,0:T(8,128)(2,1)} %get-tuple-element.987, s32[]{:T(128)S(6)} %sub.119), kind=kLoop, calls=%fused_computation.16.clone.1 | loop fusion | flops 4802560 | bytes 3325956 | tf_op jit(solution)/shard_map/while/body/eval_jaxpr/abl,bl->al/dot_general | solution.py:14
  135.9 3.0 %multiply_reduce_fusion.32 = f32[128,112]{0,1:T(8,128)S(1)} fusion(f32[128,112]{0,1:T(8,128)S(1)} %fusion.26, bf16[2,112,112,128]{3,2,1,0:T(8,128)(2,1)} %get-tuple-element.988, s32[]{:T(128)S(6)} %sub.119), kind=kLoop, calls=%fused_computation.15.clone.1 | loop fusion | flops 4802560 | bytes 3325956 | tf_op jit(solution)/shard_map/while
  139.1 2.4 %collective-permute-start.5 = (f32[112,128]{1,0:T(8,128)S(1)}, f32[112,128]{1,0:T(8,128)S(1)}, u32[]{:S(2)}, u32[]{:S(2)}) collective-permute-start(f32[112,128]{1,0:T(8,128)S(1)} %copy.13), channel_id=1, source_target_pairs={{32,0},{64,32},{96,64},{33,1},{65,33},{97,65},{34,2},{66,34},{98,6... | collective-permute-start | bytes 172040 | tf_op jit(solution)/shard_map/ppermute | solution.py:10
  141.5 3.7 %collective-permute-done.5 = f32[112,128]{1,0:T(8,128)S(1)} collective-permute-done((f32[112,128]{1,0:T(8,128)S(1)}, f32[112,128]{1,0:T(8,128)S(1)}, u32[]{:S(2)}, u32[]{:S(2)}) %collective-permute-start.5) | collective-permute-done | bytes 57376 | tf_op jit(solution)/shard_map/ppermute | solution.py:10
  145.2 12.1 %while.107 = (s32[]{:T(128)}, f32[112,128]{1,0:T(8,128)S(1)}, f32[2,112,128]{2,1,0:T(8,128)S(1)}, f32[2,112,128]{2,1,0:T(8,128)S(1)}, bf16[2,112,112,128]{3,2,1,...) while((s32[]{:T(128)}, f32[112,128]{1,0:T(8,128)S(1)}, f32[2,112,128]{2,1,0:T(8,128)S(1)}, ...), condition=%wide.region_15.16_spmd, body=%wide.region_14.15_spmd.sunk | while | flops 9619459 | bytes 6938729 | solution.py:34
  145.2 3.0 %multiply_reduce_fusion.33 = f32[128,112]{0,1:T(8,128)S(1)} fusion(f32[128,112]{0,1:T(8,128)S(1)} %bitcast.219, bf16[2,112,112,128]{3,2,1,0:T(8,128)(2,1)} %get-tuple-element.1008, s32[]{:T(128)S(6)} %sub.121), kind=kLoop, calls=%fused_computation.20.clone.1 | loop fusion | flops 4802560 | bytes 3325956 | tf_op jit(solution)/shard_map/while/body/eval_jaxpr/abl,bl->al/dot_general | solution.py:14
  148.2 3.0 %multiply_reduce_fusion.34 = f32[128,112]{0,1:T(8,128)S(1)} fusion(f32[128,112]{0,1:T(8,128)S(1)} %fusion.27, bf16[2,112,112,128]{3,2,1,0:T(8,128)(2,1)} %get-tuple-element.1009, s32[]{:T(128)S(6)} %sub.121), kind=kLoop, calls=%fused_computation.19.clone.1 | loop fusion | flops 4802560 | bytes 3325956 | tf_op jit(solution)/shard_map/while/body/eval_jaxpr/abl,bl->al/dot_general | solution.py:14
  151.3 3.0 %multiply_reduce_fusion.33 = f32[128,112]{0,1:T(8,128)S(1)} fusion(f32[128,112]{0,1:T(8,128)S(1)} %bitcast.219, bf16[2,112,112,128]{3,2,1,0:T(8,128)(2,1)} %get-tuple-element.1008, s32[]{:T(128)S(6)} %sub.121), kind=kLoop, calls=%fused_computation.20.clone.1 | loop fusion | flops 4802560 | bytes 3325956 | tf_op jit(solution)/shard_map/while/body/eval_jaxpr/abl,bl->al/dot_general | solution.py:14
  154.3 3.0 %multiply_reduce_fusion.34 = f32[128,112]{0,1:T(8,128)S(1)} fusion(f32[128,112]{0,1:T(8,128)S(1)} %fusion.27, bf16[2,112,112,128]{3,2,1,0:T(8,128)(2,1)} %get-tuple-element.1009, s32[]{:T(128)S(6)} %sub.121), kind=kLoop, calls=%fused_computation.19.clone.1 | loop fusion | flops 4802560 | bytes 3325956 | tf_op jit(solution)/shard_map/while/body/eval_jaxpr/abl,bl->al/dot_general | solution.py:14
  (53 shorter events, 6.5 us)
Async XLA Ops:
  0.0 2.3 %copy-start = (f32[2,112,128]{2,1,0:T(8,128)S(1)}, f32[2,112,128]{2,1,0:T(8,128)}, u32[]{:S(2)}) copy-start(f32[2,112,128]{2,1,0:T(8,128)} %param.29) | copy-start | bytes 344068
  0.0 13.4 %copy-start.3 = (s32[1,32,64]{2,1,0:T(8,128)S(1)}, s32[1,32,64]{2,1,0:T(8,128)}, u32[]{:S(2)}) copy-start(s32[1,32,64]{2,1,0:T(8,128)} %param.32) | copy-start | bytes 24580
  3.2 41.7 %copy-start.2 = (f32[2,112,128]{2,1,0:T(8,128)S(1)}, f32[2,112,128]{2,1,0:T(8,128)}, u32[]{:S(2)}) copy-start(f32[2,112,128]{2,1,0:T(8,128)} %param.28) | copy-start | bytes 344068
  5.1 37.2 %all-to-all-start = ((f32[224,32,64]{0,2,1:T(8,128)}), f32[224,32,64]{0,2,1:T(8,128)}, u32[]{:S(2)}, u32[]{:S(2)}) async-start(f32[224,32,64]{0,2,1:T(8,128)} %bitcast.70), calls=%async_computation | async-start | bytes 4194304 | tf_op jit(solution)/shard_map/all_to_all | solution.py:58
  53.1 6.1 %collective-permute-start = (f32[112,128]{1,0:T(8,128)S(1)}, f32[112,128]{1,0:T(8,128)S(1)}, u32[]{:S(2)}, u32[]{:S(2)}) collective-permute-start(f32[112,128]{1,0:T(8,128)S(1)} %get-tuple-element.529), channel_id=1, source_target_pairs={{0,32},{32,64},{64,96},{1,33},{33,65},{65,97},{2,34},{34,66},{66,9... | collective-permute-start | bytes 172040 | tf_op jit(solution)/shard_map/ppermute | solution.py:10
  65.2 6.1 %collective-permute-start.1 = (f32[112,128]{1,0:T(8,128)S(1)}, f32[112,128]{1,0:T(8,128)S(1)}, u32[]{:S(2)}, u32[]{:S(2)}) collective-permute-start(f32[112,128]{1,0:T(8,128)S(1)} %get-tuple-element.530), channel_id=1, source_target_pairs={{0,32},{32,64},{64,96},{1,33},{33,65},{65,97},{2,34},{34,66},{66,9... | collective-permute-start | bytes 172040 | tf_op jit(solution)/shard_map/ppermute | solution.py:10
  77.3 6.1 %collective-permute-start.2 = (f32[112,128]{1,0:T(8,128)S(1)}, f32[112,128]{1,0:T(8,128)S(1)}, u32[]{:S(2)}, u32[]{:S(2)}) collective-permute-start(f32[112,128]{1,0:T(8,128)S(1)} %get-tuple-element.531), channel_id=1, source_target_pairs={{0,32},{32,64},{64,96},{1,33},{33,65},{65,97},{2,34},{34,66},{66,9... | collective-permute-start | bytes 172040 | tf_op jit(solution)/shard_map/ppermute | solution.py:10
  101.9 6.2 %collective-permute-start.3 = (f32[112,128]{0,1:T(8,128)S(1)}, f32[112,128]{0,1:T(8,128)S(1)}, u32[]{:S(2)}, u32[]{:S(2)}) collective-permute-start(f32[112,128]{0,1:T(8,128)S(1)} %get-tuple-element.533), channel_id=1, source_target_pairs={{32,0},{64,32},{96,64},{33,1},{65,33},{97,65},{34,2},{66,34},{98,6... | collective-permute-start | bytes 172040 | tf_op jit(solution)/shard_map/ppermute | solution.py:10
  120.5 6.2 %collective-permute-start.4 = (f32[112,128]{0,1:T(8,128)S(1)}, f32[112,128]{0,1:T(8,128)S(1)}, u32[]{:S(2)}, u32[]{:S(2)}) collective-permute-start(f32[112,128]{0,1:T(8,128)S(1)} %get-tuple-element.534), channel_id=1, source_target_pairs={{32,0},{64,32},{96,64},{33,1},{65,33},{97,65},{34,2},{66,34},{98,6... | collective-permute-start | bytes 172040 | tf_op jit(solution)/shard_map/ppermute | solution.py:10
  139.1 6.1 %collective-permute-start.5 = (f32[112,128]{1,0:T(8,128)S(1)}, f32[112,128]{1,0:T(8,128)S(1)}, u32[]{:S(2)}, u32[]{:S(2)}) collective-permute-start(f32[112,128]{1,0:T(8,128)S(1)} %copy.13), channel_id=1, source_target_pairs={{32,0},{64,32},{96,64},{33,1},{65,33},{97,65},{34,2},{66,34},{98,6... | collective-permute-start | bytes 172040 | tf_op jit(solution)/shard_map/ppermute | solution.py:10
  157.3 0.6 copy-start.1
where the time goes:
time: 159 us; the launch traced here: 158 us
  other arithmetic  72.7 us (46%)
  waiting for transfers between devices  48.5 us (31%)
  starting transfers between devices  25.1 us (16%)
  local copies, waits for them, and re-layouts  7.23 us (5%)
  matrix products  3 us (2%)
    dot_general x18, other arithmetic, matvec(): jnp.einsum('abl,bl->al', block.astype(jnp.float32), vec, precision=lax.Pr...  53.7 us
    all_to_all x1, waiting for transfers between devices, local(): lax.all_to_all(outgoing, 'span', split_axis=1, concat_axis=1, tiled=True)  28.8 us
    ppermute x6, waiting for transfers between devices, from_behind(): lax.ppermute(value, axis, [(source, source + steps) for source in range(f...  19.7 us
    while x16, other arithmetic  18 us
    ppermute x6, starting transfers between devices, from_behind(): lax.ppermute(value, axis, [(source, source + steps) for source in range(f...  16.8 us
    all_to_all x1, starting transfers between devices, local(): lax.all_to_all(outgoing, 'span', split_axis=1, concat_axis=1, tiled=True)  8.29 us
  transfers between devices with their start and end apart: 7, of which 7 were waited for; matrix products, arithmetic and copies ran while one was open for 0% of the time, Pallas kernels for 0%

commit v1 on v0

--- a/solution.py
+++ b/solution.py
@@ -55,7 +55,10 @@
     picks = (lane_ids[:, None] == send_lines[0].reshape(-1)[None, :]) & keep.reshape(-1)[None, :]
     outgoing = jnp.dot(tiles, picks.astype(jnp.float32), precision=lax.Precision.HIGHEST)
     outgoing = outgoing.reshape(cells * width, spans, slot_count)
-    incoming = lax.all_to_all(outgoing, "span", split_axis=1, concat_axis=1, tiled=True)
+    incoming = jnp.concatenate(
+        lax.all_to_all(jnp.stack(jnp.split(outgoing, lax.axis_size("span"), axis=1)), "span", 0, 0),
+        axis=1,
+    )
     landing = (recv_lines[0].reshape(-1)[:, None] == lane_ids[None, :]).astype(jnp.float32)
     coupling = jnp.dot(
         incoming.reshape(cells * width, spans * slot_count),

time: 159 us -> 182 us (1.14)
  local copies, waits for them, and re-layouts: 7.23 us -> 28.6 us
    unnamed x8 -> x41, local copies, waits for them, and re-layouts: 0.65 us -> 21.3 us
where the time goes in v1:
time: 182 us; the launch traced here: 181 us
  other arithmetic  72.7 us (40%)
  waiting for transfers between devices  48.6 us (27%)
  local copies, waits for them, and re-layouts  28.6 us (16%)
  starting transfers between devices  25.1 us (14%)
  matrix products  4.26 us (2%)
    dot_general x18, other arithmetic, matvec(): jnp.einsum('abl,bl->al', block.astype(jnp.float32), vec, precision=lax.Pr...  53.7 us
    all_to_all x1, waiting for transfers between devices, local(): lax.all_to_all(jnp.stack(jnp.split(outgoing, lax.axis_size('span'), axis=...  28.8 us
    unnamed x41, local copies, waits for them, and re-layouts  21.3 us
    ppermute x6, waiting for transfers between devices, from_behind(): lax.ppermute(value, axis, [(source, source + steps) for source in range(f...  19.7 us
    while x16, other arithmetic  18 us
    ppermute x6, starting transfers between devices, from_behind(): lax.ppermute(value, axis, [(source, source + steps) for source in range(f...  16.8 us
    all_to_all x1, starting transfers between devices, local(): lax.all_to_all(jnp.stack(jnp.split(outgoing, lax.axis_size('span'), axis=...  8.3 us
  transfers between devices with their start and end apart: 7, of which 7 were waited for; matrix products, arithmetic and copies ran while one was open for 0% of the time, Pallas kernels for 0%

profile of v1, /device:TPU:16, one launch (start us, length us, event | category | flops | bytes accessed | tf_op | source)
XLA Modules:
  0.0 180.6 jit_solution(16864981496432383237)
XLA Ops:
  2.3 2.2 %convolution_bitcast_fusion = f32[224,2048]{1,0:T(8,128)} fusion(f32[224,128]{1,0:T(8,128)S(1)} %bitcast.349, s32[2048]{0:T(1024)S(1)} %eq.31, pred[2048]{0:T(1024)(128)(4,1)S(1)} %compare_and_fusion), kind=kOutput, calls=%fused_computation.27 | convolution fusion | flops 705167360 | bytes 1959936 | tf_op jit(solution)/shard_map/dot_general | solution.py:56
  26.3 8.3 %all-to-all-start = ((f32[32,224,1,64]{1,3,2,0:T(8,128)}), f32[32,224,1,64]{1,3,2,0:T(8,128)S(1)}, u32[]{:S(2)}, u32[]{:S(2)}) async-start(f32[32,224,1,64]{1,3,2,0:T(8,128)} %constant_dynamic-update-slice_fusion), calls=%async_computation | async-start | bytes 4194304 | tf_op jit(solution)/shard_map/all_to_all | solution.py:59
  34.7 28.8 %all-to-all-done = f32[32,224,1,64]{1,3,2,0:T(8,128)S(1)} async-done(((f32[32,224,1,64]{1,3,2,0:T(8,128)}), f32[32,224,1,64]{1,3,2,0:T(8,128)S(1)}, u32[]{:S(2)}, u32[]{:S(2)}) %all-to-all-start) | async-done | bytes 1835040 | tf_op jit(solution)/shard_map/all_to_all | solution.py:59
  64.9 2.7 %dot_general.72 = f32[2,112,2048]{1,0,2:T(2,128)S(1)} reshape(f32[224,32,1,64]{0,3,2,1:T(8,128)} %bitcast.382) | data formatting | bytes 3670016 | tf_op jit(solution)/shard_map/dot_general | solution.py:63
  69.7 6.1 %while.108 = (s32[]{:T(128)}, f32[112,128]{1,0:T(8,128)S(1)}, f32[2,112,128]{2,1,0:T(8,128)S(1)}, bf16[2,112,112,128]{3,2,1,0:T(8,128)(2,1)}, s32[]{:T(128)}, /*index=5*/s32[]{:T(128)}) while((s32[]{:T(128)}, f32[112,128]{1,0:T(8,128)S(1)}, f32[2,112,128]{2,1,0:T(8,128)S(1)}, bf16[2,112,112,128]{3,2,1,0:T(8,128)(2,1)}, s32[]{:T(128)}, ...), condition=%wide.region_1.2_spmd.clone, body=%wide.region_0.1_spmd.clone.sunk | while | flops 4831235 | bytes 3612759 | solution.py:24
  69.7 3.0 %multiply_reduce_fusion.35 = f32[128,112]{0,1:T(8,128)S(1)} fusion(f32[128,112]{0,1:T(8,128)S(1)} %select_bitcast_fusion.2, bf16[2,112,112,128]{3,2,1,0:T(8,128)(2,1)} %get-tuple-element.885, s32[]{:T(128)} %get-tuple-element.876), kind=kLoop, calls=%fused_computation.24.clone.1 | loop fusion | flops 4802560 | bytes 3325956 | tf_op jit(solution)/shard_map/while/body/eval_jaxpr/abl,bl->al/dot_general | solution.py:14
  72.8 3.0 %multiply_reduce_fusion.35 = f32[128,112]{0,1:T(8,128)S(1)} fusion(f32[128,112]{0,1:T(8,128)S(1)} %select_bitcast_fusion.2, bf16[2,112,112,128]{3,2,1,0:T(8,128)(2,1)} %get-tuple-element.885, s32[]{:T(128)} %get-tuple-element.876), kind=kLoop, calls=%fused_computation.24.clone.1 | loop fusion | flops 4802560 | bytes 3325956 | tf_op jit(solution)/shard_map/while/body/eval_jaxpr/abl,bl->al/dot_general | solution.py:14
  75.8 3.2 %collective-permute-start = (f32[112,128]{1,0:T(8,128)S(1)}, f32[112,128]{1,0:T(8,128)S(1)}, u32[]{:S(2)}, u32[]{:S(2)}) collective-permute-start(f32[112,128]{1,0:T(8,128)S(1)} %get-tuple-element.529), channel_id=1, source_target_pairs={{0,32},{32,64},{64,96},{1,33},{33,65},{65,97},{2,34},{34,66},{66,9... | collective-permute-start | bytes 172040 | tf_op jit(solution)/shard_map/ppermute | solution.py:10
  79.0 2.9 %collective-permute-done = f32[112,128]{1,0:T(8,128)S(1)} collective-permute-done((f32[112,128]{1,0:T(8,128)S(1)}, f32[112,128]{1,0:T(8,128)S(1)}, u32[]{:S(2)}, u32[]{:S(2)}) %collective-permute-start) | collective-permute-done | bytes 57376 | tf_op jit(solution)/shard_map/ppermute | solution.py:10
  81.8 6.0 %while.101 = (s32[]{:T(128)}, f32[112,128]{1,0:T(8,128)S(1)}, f32[2,112,128]{2,1,0:T(8,128)S(1)}, bf16[2,112,112,128]{3,2,1,0:T(8,128)(2,1)}, s32[]{:T(128)}) while((s32[]{:T(128)}, f32[112,128]{1,0:T(8,128)S(1)}, f32[2,112,128]{2,1,0:T(8,128)S(1)}, bf16[2,112,112,128]{3,2,1,0:T(8,128)(2,1)}, s32[]{:T(128)}) %tuple.213), condition=%wide.region_3.4_spmd, body=%wide.region_2.3_spmd.sunk | while | flops 4816898 | bytes 3498053 | solution.py:24
  81.8 3.0 %multiply_reduce_fusion.24 = f32[128,112]{0,1:T(8,128)S(1)} fusion(f32[128,112]{0,1:T(8,128)S(1)} %bitcast.392, bf16[2,112,112,128]{3,2,1,0:T(8,128)(2,1)} %get-tuple-element.901, s32[]{:T(128)} %get-tuple-element.893), kind=kLoop, calls=%fused_computation.clone.1 | loop fusion | flops 4802560 | bytes 3325956 | tf_op jit(solution)/shard_map/while/body/eval_jaxpr/abl,bl->al/dot_general | solution.py:14
  84.9 3.0 %multiply_reduce_fusion.24 = f32[128,112]{0,1:T(8,128)S(1)} fusion(f32[128,112]{0,1:T(8,128)S(1)} %bitcast.392, bf16[2,112,112,128]{3,2,1,0:T(8,128)(2,1)} %get-tuple-element.901, s32[]{:T(128)} %get-tuple-element.893), kind=kLoop, calls=%fused_computation.clone.1 | loop fusion | flops 4802560 | bytes 3325956 | tf_op jit(solution)/shard_map/while/body/eval_jaxpr/abl,bl->al/dot_general | solution.py:14
  87.9 3.2 %collective-permute-start.1 = (f32[112,128]{1,0:T(8,128)S(1)}, f32[112,128]{1,0:T(8,128)S(1)}, u32[]{:S(2)}, u32[]{:S(2)}) collective-permute-start(f32[112,128]{1,0:T(8,128)S(1)} %get-tuple-element.530), channel_id=1, source_target_pairs={{0,32},{32,64},{64,96},{1,33},{33,65},{65,97},{2,34},{34,66},{66,9... | collective-permute-start | bytes 172040 | tf_op jit(solution)/shard_map/ppermute | solution.py:10
  91.1 2.9 %collective-permute-done.1 = f32[112,128]{1,0:T(8,128)S(1)} collective-permute-done((f32[112,128]{1,0:T(8,128)S(1)}, f32[112,128]{1,0:T(8,128)S(1)}, u32[]{:S(2)}, u32[]{:S(2)}) %collective-permute-start.1) | collective-permute-done | bytes 57376 | tf_op jit(solution)/shard_map/ppermute | solution.py:10
  94.0 6.0 %while.102 = (s32[]{:T(128)}, f32[112,128]{1,0:T(8,128)S(1)}, f32[2,112,128]{2,1,0:T(8,128)S(1)}, bf16[2,112,112,128]{3,2,1,0:T(8,128)(2,1)}, s32[]{:T(128)}) while((s32[]{:T(128)}, f32[112,128]{1,0:T(8,128)S(1)}, f32[2,112,128]{2,1,0:T(8,128)S(1)}, bf16[2,112,112,128]{3,2,1,0:T(8,128)(2,1)}, s32[]{:T(128)}) %tuple.214), condition=%wide.region_5.6_spmd, body=%wide.region_4.5_spmd.sunk | while | flops 4816898 | bytes 3498053 | solution.py:24
  94.0 3.0 %multiply_reduce_fusion.25 = f32[128,112]{0,1:T(8,128)S(1)} fusion(f32[128,112]{0,1:T(8,128)S(1)} %bitcast.393, bf16[2,112,112,128]{3,2,1,0:T(8,128)(2,1)} %get-tuple-element.916, s32[]{:T(128)} %get-tuple-element.908), kind=kLoop, calls=%fused_computation.2.clone.1 | loop fusion | flops 4802560 | bytes 3325956 | tf_op jit(solution)/shard_map/while/body/eval_jaxpr/abl,bl->al/dot_general | solution.py:14
  97.0 3.0 %multiply_reduce_fusion.25 = f32[128,112]{0,1:T(8,128)S(1)} fusion(f32[128,112]{0,1:T(8,128)S(1)} %bitcast.393, bf16[2,112,112,128]{3,2,1,0:T(8,128)(2,1)} %get-tuple-element.916, s32[]{:T(128)} %get-tuple-element.908), kind=kLoop, calls=%fused_computation.2.clone.1 | loop fusion | flops 4802560 | bytes 3325956 | tf_op jit(solution)/shard_map/while/body/eval_jaxpr/abl,bl->al/dot_general | solution.py:14
  100.0 3.4 %collective-permute-start.2 = (f32[112,128]{1,0:T(8,128)S(1)}, f32[112,128]{1,0:T(8,128)S(1)}, u32[]{:S(2)}, u32[]{:S(2)}) collective-permute-start(f32[112,128]{1,0:T(8,128)S(1)} %get-tuple-element.531), channel_id=1, source_target_pairs={{0,32},{32,64},{64,96},{1,33},{33,65},{65,97},{2,34},{34,66},{66,9... | collective-permute-start | bytes 172040 | tf_op jit(solution)/shard_map/ppermute | solution.py:10
  103.4 2.7 %collective-permute-done.2 = f32[112,128]{1,0:T(8,128)S(1)} collective-permute-done((f32[112,128]{1,0:T(8,128)S(1)}, f32[112,128]{1,0:T(8,128)S(1)}, u32[]{:S(2)}, u32[]{:S(2)}) %collective-permute-start.2) | collective-permute-done | bytes 57376 | tf_op jit(solution)/shard_map/ppermute | solution.py:10
  106.1 6.1 %while.103 = (s32[]{:T(128)}, f32[112,128]{1,0:T(8,128)S(1)}, f32[2,112,128]{2,1,0:T(8,128)S(1)}, f32[2,112,128]{2,1,0:T(8,128)S(1)}, bf16[2,112,112,128]{3,2,1,0:T(8,128)(2,1)}, /*index=5*/s32[]{:T(128)}) while((s32[]{:T(128)}, f32[112,128]{1,0:T(8,128)S(1)}, f32[2,112,128]{2,1,0:T(8,128)S(1)}, f32[2,112,128]{2,1,0:T(8,128)S(1)}, ...), condition=%wide.region_7.8_spmd, body=%wide.region_6.7_spmd.sunk | while | flops 4816898 | bytes 3555405 | solution.py:24
  106.1 3.0 %multiply_reduce_fusion.26 = f32[128,112]{0,1:T(8,128)S(1)} fusion(f32[128,112]{0,1:T(8,128)S(1)} %bitcast.391, bf16[2,112,112,128]{3,2,1,0:T(8,128)(2,1)} %get-tuple-element.934, s32[]{:T(128)} %get-tuple-element.924), kind=kLoop, calls=%fused_computation.4.clone.1 | loop fusion | flops 4802560 | bytes 3325956 | tf_op jit(solution)/shard_map/while/body/eval_jaxpr/abl,bl->al/dot_general | solution.py:14
  109.1 3.0 %multiply_reduce_fusion.26 = f32[128,112]{0,1:T(8,128)S(1)} fusion(f32[128,112]{0,1:T(8,128)S(1)} %bitcast.391, bf16[2,112,112,128]{3,2,1,0:T(8,128)(2,1)} %get-tuple-element.934, s32[]{:T(128)} %get-tuple-element.924), kind=kLoop, calls=%fused_computation.4.clone.1 | loop fusion | flops 4802560 | bytes 3325956 | tf_op jit(solution)/shard_map/while/body/eval_jaxpr/abl,bl->al/dot_general | solution.py:14
  112.2 12.4 %while.104 = (s32[]{:T(128)}, f32[112,128]{0,1:T(8,128)S(1)}, f32[2,112,128]{2,1,0:T(8,128)S(1)}, bf16[2,112,112,128]{3,2,1,0:T(8,128)(2,1)}, bf16[2,112,112,128]{3,2,1,0:T(8,128)(2,1)}, /*index=5*/s32[]{:T(128)}) while((s32[]{:T(128)}, f32[112,128]{0,1:T(8,128)S(1)}, f32[2,112,128]{2,1,0:T(8,128)S(1)}, bf16[2,112,112,128]{3,2,1,0:T(8,128)(2,1)}, ...), condition=%wide.region_9.10_spmd, body=%wide.region_8.9_spmd.sunk | while | flops 9619459 | bytes 7053405 | solution.py:34
  112.3 3.0 %multiply_reduce_fusion.27 = f32[128,112]{0,1:T(8,128)S(1)} fusion(f32[128,112]{0,1:T(8,128)S(1)} %copy.151, bf16[2,112,112,128]{3,2,1,0:T(8,128)(2,1)} %get-tuple-element.951, s32[]{:T(128)S(6)} %sub.115), kind=kLoop, calls=%fused_computation.8.clone.1 | loop fusion | flops 4802560 | bytes 3325956 | tf_op jit(solution)/shard_map/while/body/eval_jaxpr/abl,bl->al/dot_general | solution.py:14
  115.3 3.0 %multiply_reduce_fusion.28 = f32[128,112]{0,1:T(8,128)S(1)} fusion(f32[128,112]{0,1:T(8,128)S(1)} %fusion.24, bf16[2,112,112,128]{3,2,1,0:T(8,128)(2,1)} %get-tuple-element.952, s32[]{:T(128)S(6)} %sub.115), kind=kLoop, calls=%fused_computation.7.clone.1 | loop fusion | flops 4802560 | bytes 3325956 | tf_op jit(solution)/shard_map/while
  118.5 3.0 %multiply_reduce_fusion.27 = f32[128,112]{0,1:T(8,128)S(1)} fusion(f32[128,112]{0,1:T(8,128)S(1)} %copy.151, bf16[2,112,112,128]{3,2,1,0:T(8,128)(2,1)} %get-tuple-element.951, s32[]{:T(128)S(6)} %sub.115), kind=kLoop, calls=%fused_computation.8.clone.1 | loop fusion | flops 4802560 | bytes 3325956 | tf_op jit(solution)/shard_map/while/body/eval_jaxpr/abl,bl->al/dot_general | solution.py:14
  121.5 3.0 %multiply_reduce_fusion.28 = f32[128,112]{0,1:T(8,128)S(1)} fusion(f32[128,112]{0,1:T(8,128)S(1)} %fusion.24, bf16[2,112,112,128]{3,2,1,0:T(8,128)(2,1)} %get-tuple-element.952, s32[]{:T(128)S(6)} %sub.115), kind=kLoop, calls=%fused_computation.7.clone.1 | loop fusion | flops 4802560 | bytes 3325956 | tf_op jit(solution)/shard_map/while
  124.6 2.4 %collective-permute-start.3 = (f32[112,128]{0,1:T(8,128)S(1)}, f32[112,128]{0,1:T(8,128)S(1)}, u32[]{:S(2)}, u32[]{:S(2)}) collective-permute-start(f32[112,128]{0,1:T(8,128)S(1)} %get-tuple-element.533), channel_id=1, source_target_pairs={{32,0},{64,32},{96,64},{33,1},{65,33},{97,65},{34,2},{66,34},{98,6... | collective-permute-start | bytes 172040 | tf_op jit(solution)/shard_map/ppermute | solution.py:10
  127.0 3.8 %collective-permute-done.3 = f32[112,128]{0,1:T(8,128)S(1)} collective-permute-done((f32[112,128]{0,1:T(8,128)S(1)}, f32[112,128]{0,1:T(8,128)S(1)}, u32[]{:S(2)}, u32[]{:S(2)}) %collective-permute-start.3) | collective-permute-done | bytes 57376 | tf_op jit(solution)/shard_map/ppermute | solution.py:10
  130.7 12.4 %while.105 = (s32[]{:T(128)}, f32[112,128]{0,1:T(8,128)S(1)}, f32[2,112,128]{2,1,0:T(8,128)S(1)}, bf16[2,112,112,128]{3,2,1,0:T(8,128)(2,1)}, bf16[2,112,112,128]{3,2,1,0:T(8,128)(2,1)}, /*index=5*/s32[]{:T(128)}) while((s32[]{:T(128)}, f32[112,128]{0,1:T(8,128)S(1)}, f32[2,112,128]{2,1,0:T(8,128)S(1)}, ...), condition=%wide.region_11.12_spmd, body=%wide.region_10.11_spmd.sunk | while | flops 9619459 | bytes 7053405 | solution.py:34
  130.8 3.0 %multiply_reduce_fusion.29 = f32[128,112]{0,1:T(8,128)S(1)} fusion(f32[128,112]{0,1:T(8,128)S(1)} %copy.153, bf16[2,112,112,128]{3,2,1,0:T(8,128)(2,1)} %get-tuple-element.969, s32[]{:T(128)S(6)} %sub.117), kind=kLoop, calls=%fused_computation.12.clone.1 | loop fusion | flops 4802560 | bytes 3325956 | tf_op jit(solution)/shard_map/while/body/eval_jaxpr/abl,bl->al/dot_general | solution.py:14
  133.8 3.0 %multiply_reduce_fusion.30 = f32[128,112]{0,1:T(8,128)S(1)} fusion(f32[128,112]{0,1:T(8,128)S(1)} %fusion.25, bf16[2,112,112,128]{3,2,1,0:T(8,128)(2,1)} %get-tuple-element.970, s32[]{:T(128)S(6)} %sub.117), kind=kLoop, calls=%fused_computation.11.clone.1 | loop fusion | flops 4802560 | bytes 3325956 | tf_op jit(solution)/shard_map/while
  137.0 3.0 %multiply_reduce_fusion.29 = f32[128,112]{0,1:T(8,128)S(1)} fusion(f32[128,112]{0,1:T(8,128)S(1)} %copy.153, bf16[2,112,112,128]{3,2,1,0:T(8,128)(2,1)} %get-tuple-element.969, s32[]{:T(128)S(6)} %sub.117), kind=kLoop, calls=%fused_computation.12.clone.1 | loop fusion | flops 4802560 | bytes 3325956 | tf_op jit(solution)/shard_map/while/body/eval_jaxpr/abl,bl->al/dot_general | solution.py:14
  140.1 3.0 %multiply_reduce_fusion.30 = f32[128,112]{0,1:T(8,128)S(1)} fusion(f32[128,112]{0,1:T(8,128)S(1)} %fusion.25, bf16[2,112,112,128]{3,2,1,0:T(8,128)(2,1)} %get-tuple-element.970, s32[]{:T(128)S(6)} %sub.117), kind=kLoop, calls=%fused_computation.11.clone.1 | loop fusion | flops 4802560 | bytes 3325956 | tf_op jit(solution)/shard_map/while
  143.1 2.4 %collective-permute-start.4 = (f32[112,128]{0,1:T(8,128)S(1)}, f32[112,128]{0,1:T(8,128)S(1)}, u32[]{:S(2)}, u32[]{:S(2)}) collective-permute-start(f32[112,128]{0,1:T(8,128)S(1)} %get-tuple-element.534), channel_id=1, source_target_pairs={{32,0},{64,32},{96,64},{33,1},{65,33},{97,65},{34,2},{66,34},{98,6... | collective-permute-start | bytes 172040 | tf_op jit(solution)/shard_map/ppermute | solution.py:10
  145.5 3.8 %collective-permute-done.4 = f32[112,128]{0,1:T(8,128)S(1)} collective-permute-done((f32[112,128]{0,1:T(8,128)S(1)}, f32[112,128]{0,1:T(8,128)S(1)}, u32[]{:S(2)}, u32[]{:S(2)}) %collective-permute-start.4) | collective-permute-done | bytes 57376 | tf_op jit(solution)/shard_map/ppermute | solution.py:10
  149.3 12.4 %while.106 = (s32[]{:T(128)}, f32[112,128]{0,1:T(8,128)S(1)}, f32[2,112,128]{2,1,0:T(8,128)S(1)}, bf16[2,112,112,128]{3,2,1,0:T(8,128)(2,1)}, bf16[2,112,112,128]{3,2,1,0:T(8,128)(2,1)}, /*index=5*/s32[]{:T(128)}) while((s32[]{:T(128)}, f32[112,128]{0,1:T(8,128)S(1)}, f32[2,112,128]{2,1,0:T(8,128)S(1)}, ...), condition=%wide.region_13.14_spmd, body=%wide.region_12.13_spmd.sunk | while | flops 9619459 | bytes 7053405 | solution.py:34
  149.4 3.0 %multiply_reduce_fusion.31 = f32[128,112]{0,1:T(8,128)S(1)} fusion(f32[128,112]{0,1:T(8,128)S(1)} %copy.155, bf16[2,112,112,128]{3,2,1,0:T(8,128)(2,1)} %get-tuple-element.987, s32[]{:T(128)S(6)} %sub.119), kind=kLoop, calls=%fused_computation.16.clone.1 | loop fusion | flops 4802560 | bytes 3325956 | tf_op jit(solution)/shard_map/while/body/eval_jaxpr/abl,bl->al/dot_general | solution.py:14
  152.4 3.0 %multiply_reduce_fusion.32 = f32[128,112]{0,1:T(8,128)S(1)} fusion(f32[128,112]{0,1:T(8,128)S(1)} %fusion.26, bf16[2,112,112,128]{3,2,1,0:T(8,128)(2,1)} %get-tuple-element.988, s32[]{:T(128)S(6)} %sub.119), kind=kLoop, calls=%fused_computation.15.clone.1 | loop fusion | flops 4802560 | bytes 3325956 | tf_op jit(solution)/shard_map/while
  155.6 3.0 %multiply_reduce_fusion.31 = f32[128,112]{0,1:T(8,128)S(1)} fusion(f32[128,112]{0,1:T(8,128)S(1)} %copy.155, bf16[2,112,112,128]{3,2,1,0:T(8,128)(2,1)} %get-tuple-element.987, s32[]{:T(128)S(6)} %sub.119), kind=kLoop, calls=%fused_computation.16.clone.1 | loop fusion | flops 4802560 | bytes 3325956 | tf_op jit(solution)/shard_map/while/body/eval_jaxpr/abl,bl->al/dot_general | solution.py:14
  158.6 3.0 %multiply_reduce_fusion.32 = f32[128,112]{0,1:T(8,128)S(1)} fusion(f32[128,112]{0,1:T(8,128)S(1)} %fusion.26, bf16[2,112,112,128]{3,2,1,0:T(8,128)(2,1)} %get-tuple-element.988, s32[]{:T(128)S(6)} %sub.119), kind=kLoop, calls=%fused_computation.15.clone.1 | loop fusion | flops 4802560 | bytes 3325956 | tf_op jit(solution)/shard_map/while
  161.8 2.4 %collective-permute-start.5 = (f32[112,128]{1,0:T(8,128)S(1)}, f32[112,128]{1,0:T(8,128)S(1)}, u32[]{:S(2)}, u32[]{:S(2)}) collective-permute-start(f32[112,128]{1,0:T(8,128)S(1)} %copy.45), channel_id=1, source_target_pairs={{32,0},{64,32},{96,64},{33,1},{65,33},{97,65},{34,2},{66,34},{98,6... | collective-permute-start | bytes 172040 | tf_op jit(solution)/shard_map/ppermute | solution.py:10
  164.2 3.7 %collective-permute-done.5 = f32[112,128]{1,0:T(8,128)S(1)} collective-permute-done((f32[112,128]{1,0:T(8,128)S(1)}, f32[112,128]{1,0:T(8,128)S(1)}, u32[]{:S(2)}, u32[]{:S(2)}) %collective-permute-start.5) | collective-permute-done | bytes 57376 | tf_op jit(solution)/shard_map/ppermute | solution.py:10
  167.9 12.1 %while.107 = (s32[]{:T(128)}, f32[112,128]{1,0:T(8,128)S(1)}, f32[2,112,128]{2,1,0:T(8,128)S(1)}, f32[2,112,128]{2,1,0:T(8,128)S(1)}, bf16[2,112,112,128]{3,2,1,...) while((s32[]{:T(128)}, f32[112,128]{1,0:T(8,128)S(1)}, f32[2,112,128]{2,1,0:T(8,128)S(1)}, ...), condition=%wide.region_15.16_spmd, body=%wide.region_14.15_spmd.sunk | while | flops 9619459 | bytes 6938729 | solution.py:34
  167.9 3.0 %multiply_reduce_fusion.33 = f32[128,112]{0,1:T(8,128)S(1)} fusion(f32[128,112]{0,1:T(8,128)S(1)} %bitcast.383, bf16[2,112,112,128]{3,2,1,0:T(8,128)(2,1)} %get-tuple-element.1008, s32[]{:T(128)S(6)} %sub.121), kind=kLoop, calls=%fused_computation.20.clone.1 | loop fusion | flops 4802560 | bytes 3325956 | tf_op jit(solution)/shard_map/while/body/eval_jaxpr/abl,bl->al/dot_general | solution.py:14
  170.9 3.0 %multiply_reduce_fusion.34 = f32[128,112]{0,1:T(8,128)S(1)} fusion(f32[128,112]{0,1:T(8,128)S(1)} %fusion.27, bf16[2,112,112,128]{3,2,1,0:T(8,128)(2,1)} %get-tuple-element.1009, s32[]{:T(128)S(6)} %sub.121), kind=kLoop, calls=%fused_computation.19.clone.1 | loop fusion | flops 4802560 | bytes 3325956 | tf_op jit(solution)/shard_map/while/body/eval_jaxpr/abl,bl->al/dot_general | solution.py:14
  173.9 3.0 %multiply_reduce_fusion.33 = f32[128,112]{0,1:T(8,128)S(1)} fusion(f32[128,112]{0,1:T(8,128)S(1)} %bitcast.383, bf16[2,112,112,128]{3,2,1,0:T(8,128)(2,1)} %get-tuple-element.1008, s32[]{:T(128)S(6)} %sub.121), kind=kLoop, calls=%fused_computation.20.clone.1 | loop fusion | flops 4802560 | bytes 3325956 | tf_op jit(solution)/shard_map/while/body/eval_jaxpr/abl,bl->al/dot_general | solution.py:14
  176.9 3.0 %multiply_reduce_fusion.34 = f32[128,112]{0,1:T(8,128)S(1)} fusion(f32[128,112]{0,1:T(8,128)S(1)} %fusion.27, bf16[2,112,112,128]{3,2,1,0:T(8,128)(2,1)} %get-tuple-element.1009, s32[]{:T(128)S(6)} %sub.121), kind=kLoop, calls=%fused_computation.19.clone.1 | loop fusion | flops 4802560 | bytes 3325956 | tf_op jit(solution)/shard_map/while/body/eval_jaxpr/abl,bl->al/dot_general | solution.py:14
  (87 shorter events, 29.0 us)
Async XLA Ops:
  0.0 2.3 %copy-start = (f32[2,112,128]{2,1,0:T(8,128)S(1)}, f32[2,112,128]{2,1,0:T(8,128)}, u32[]{:S(2)}) copy-start(f32[2,112,128]{2,1,0:T(8,128)} %param.29) | copy-start | bytes 344068
  26.3 8.3 %copy-start.4 = (s32[1,32,64]{2,1,0:T(8,128)S(1)}, s32[1,32,64]{2,1,0:T(8,128)}, u32[]{:S(2)}) copy-start(s32[1,32,64]{2,1,0:T(8,128)} %param.32) | copy-start | bytes 24580
  26.3 37.2 %all-to-all-start = ((f32[32,224,1,64]{1,3,2,0:T(8,128)}), f32[32,224,1,64]{1,3,2,0:T(8,128)S(1)}, u32[]{:S(2)}, u32[]{:S(2)}) async-start(f32[32,224,1,64]{1,3,2,0:T(8,128)} %constant_dynamic-update-slice_fusion), calls=%async_computation | async-start | bytes 4194304 | tf_op jit(solution)/shard_map/all_to_all | solution.py:59
  63.5 1.4 copy-start.1
  64.9 2.7 %copy-start.3 = (f32[2,112,128]{2,1,0:T(8,128)S(1)}, f32[2,112,128]{2,1,0:T(8,128)}, u32[]{:S(2)}) copy-start(f32[2,112,128]{2,1,0:T(8,128)} %param.28) | copy-start | bytes 344068
  75.8 6.1 %collective-permute-start = (f32[112,128]{1,0:T(8,128)S(1)}, f32[112,128]{1,0:T(8,128)S(1)}, u32[]{:S(2)}, u32[]{:S(2)}) collective-permute-start(f32[112,128]{1,0:T(8,128)S(1)} %get-tuple-element.529), channel_id=1, source_target_pairs={{0,32},{32,64},{64,96},{1,33},{33,65},{65,97},{2,34},{34,66},{66,9... | collective-permute-start | bytes 172040 | tf_op jit(solution)/shard_map/ppermute | solution.py:10
  87.9 6.1 %collective-permute-start.1 = (f32[112,128]{1,0:T(8,128)S(1)}, f32[112,128]{1,0:T(8,128)S(1)}, u32[]{:S(2)}, u32[]{:S(2)}) collective-permute-start(f32[112,128]{1,0:T(8,128)S(1)} %get-tuple-element.530), channel_id=1, source_target_pairs={{0,32},{32,64},{64,96},{1,33},{33,65},{65,97},{2,34},{34,66},{66,9... | collective-permute-start | bytes 172040 | tf_op jit(solution)/shard_map/ppermute | solution.py:10
  100.0 6.1 %collective-permute-start.2 = (f32[112,128]{1,0:T(8,128)S(1)}, f32[112,128]{1,0:T(8,128)S(1)}, u32[]{:S(2)}, u32[]{:S(2)}) collective-permute-start(f32[112,128]{1,0:T(8,128)S(1)} %get-tuple-element.531), channel_id=1, source_target_pairs={{0,32},{32,64},{64,96},{1,33},{33,65},{65,97},{2,34},{34,66},{66,9... | collective-permute-start | bytes 172040 | tf_op jit(solution)/shard_map/ppermute | solution.py:10
  124.6 6.2 %collective-permute-start.3 = (f32[112,128]{0,1:T(8,128)S(1)}, f32[112,128]{0,1:T(8,128)S(1)}, u32[]{:S(2)}, u32[]{:S(2)}) collective-permute-start(f32[112,128]{0,1:T(8,128)S(1)} %get-tuple-element.533), channel_id=1, source_target_pairs={{32,0},{64,32},{96,64},{33,1},{65,33},{97,65},{34,2},{66,34},{98,6... | collective-permute-start | bytes 172040 | tf_op jit(solution)/shard_map/ppermute | solution.py:10
  143.1 6.2 %collective-permute-start.4 = (f32[112,128]{0,1:T(8,128)S(1)}, f32[112,128]{0,1:T(8,128)S(1)}, u32[]{:S(2)}, u32[]{:S(2)}) collective-permute-start(f32[112,128]{0,1:T(8,128)S(1)} %get-tuple-element.534), channel_id=1, source_target_pairs={{32,0},{64,32},{96,64},{33,1},{65,33},{97,65},{34,2},{66,34},{98,6... | collective-permute-start | bytes 172040 | tf_op jit(solution)/shard_map/ppermute | solution.py:10
  161.8 6.1 %collective-permute-start.5 = (f32[112,128]{1,0:T(8,128)S(1)}, f32[112,128]{1,0:T(8,128)S(1)}, u32[]{:S(2)}, u32[]{:S(2)}) collective-permute-start(f32[112,128]{1,0:T(8,128)S(1)} %copy.45), channel_id=1, source_target_pairs={{32,0},{64,32},{96,64},{33,1},{65,33},{97,65},{34,2},{66,34},{98,6... | collective-permute-start | bytes 172040 | tf_op jit(solution)/shard_map/ppermute | solution.py:10
  180.0 0.6 copy-start.2
